TPU v7x, 32 devices: a whole 2x2x4 slice. The times are simulated.
32 devices in a mesh: section: 2 (over y), expert: 16 (over z, x, core).
Axes of the slice: x: 2, y: 2, z: 4, core: 2. Of those that a mesh axis runs over, the one named last changes fastest.
Arguments:
- act_fwd: bfloat16 [2, 2048, 4096], P('section', 'expert'), may hold values from -6 to 6
- act_rev: bfloat16 [2, 2048, 4096], P('section', 'expert'), may hold values from -6 to 6
- ids_fwd: int32 [2, 2048, 2], P('section', 'expert'), may hold values from 0 to 7, all different within a row; in each aligned block of 128 rows (0 to 127, 128 to 255, ..., all dimensions but the last counted through in order) at most 48 rows name the same one
- ids_rev: int32 [2, 2048, 2], P('section', 'expert'), may hold values from 0 to 7, all different within a row; in each aligned block of 128 rows (0 to 127, 128 to 255, ..., all dimensions but the last counted through in order) at most 48 rows name the same one
- probs_fwd: float32 [2, 2048, 2], P('section', 'expert'), may hold values from 0.05 to 1
- probs_rev: float32 [2, 2048, 2], P('section', 'expert'), may hold values from 0.05 to 1
- w_gate: bfloat16 [2, 4096, 6144], P('section', None, 'expert'), may hold values from -0.09375 to 0.09375
- w_up: bfloat16 [2, 4096, 6144], P('section', None, 'expert'), may hold values from -0.09375 to 0.09375
- w_down: bfloat16 [2, 6144, 4096], P('section', 'expert'), may hold values from -0.21875 to 0.21875
Outputs:
- out_fwd: bfloat16 [2, 2048, 4096], P('section', 'expert')
- out_rev: bfloat16 [2, 2048, 4096], P('section', 'expert')
Inputs may be any that keep to these rules, and one draw needn't show every extreme that they name: `ids_fwd`: each row names 2 different experts. Within the 128 rows of one device (aligned blocks) no expert is named by more than 48 rows, and some block reaches 48. `ids_rev`: as for ids_fwd.
All inputs are finite; a program needn't handle non-finite values.
Results may differ from a plain program's by a relative error of at most 0.0048.
Values may be sent and summed in bfloat16 or wider, within the bound.
A program may use at most 128 MiB of HBM per device.

v0:
```python
import jax
import jax.numpy as jnp
from jax import lax
from jax.sharding import PartitionSpec as P


def from_behind(block, axis, distance):
    devices = range(lax.axis_size(axis))
    route = [((i - distance) % len(devices), i) for i in devices]
    return lax.ppermute(block, axis, route)


def expert_rows(received_rows, w_gate, w_up, w_down):
    model_width = received_rows.shape[-1]
    flat_rows = received_rows.reshape(-1, model_width)
    gate_pre = jnp.dot(flat_rows, w_gate[0], preferred_element_type=jnp.float32)
    up_pre = jnp.dot(flat_rows, w_up[0], preferred_element_type=jnp.float32)
    hidden = (jax.nn.silu(gate_pre) * up_pre).astype(jnp.bfloat16)
    partial_value = jnp.dot(hidden, w_down[0], preferred_element_type=jnp.float32).astype(
        jnp.bfloat16
    )
    return partial_value.reshape(received_rows.shape)


def moe_layer(tokens_in, route_ids, probs, w_gate, w_up, w_down):
    tok_count, route_count = route_ids.shape
    model_width = tokens_in.shape[1]
    device_count = lax.axis_size("expert")
    expert_count = device_count // 2
    slot_count = 2 * (3 * tok_count * route_count // (4 * expert_count))
    flat_ids = route_ids.reshape(-1)
    one_hot = (flat_ids[:, None] == jnp.arange(expert_count, dtype=jnp.int32)[None, :]).astype(
        jnp.int32
    )
    rank_in = jnp.sum((jnp.cumsum(one_hot, axis=0) - 1) * one_hot, axis=1)
    slot_of = flat_ids * slot_count + rank_in
    slot_range = jnp.arange(expert_count * slot_count, dtype=jnp.int32)
    pick_rows = (slot_range[:, None] == slot_of[None, :]).astype(jnp.bfloat16)
    pick_tokens = jnp.sum(
        pick_rows.reshape(expert_count * slot_count, tok_count, route_count), axis=2
    )
    outgoing = jnp.dot(pick_tokens, tokens_in, preferred_element_type=jnp.float32).astype(
        jnp.bfloat16
    )
    outgoing_all = jnp.repeat(outgoing.reshape(expert_count, slot_count, model_width), 2, axis=0)
    partial_value = expert_rows(
        lax.all_to_all(outgoing_all, "expert", split_axis=0, concat_axis=0, tiled=True),
        w_gate,
        w_up,
        w_down,
    )
    returned = lax.all_to_all(partial_value, "expert", split_axis=0, concat_axis=0, tiled=True)
    paired_sum = jnp.sum(
        returned.reshape(expert_count, 2, slot_count, model_width).astype(jnp.float32), axis=1
    )
    expert_out = paired_sum.astype(jnp.bfloat16).reshape(expert_count * slot_count, model_width)
    route_pick = (slot_of[:, None] == slot_range[None, :]).astype(jnp.bfloat16)
    per_route = jnp.dot(route_pick, expert_out, preferred_element_type=jnp.float32)
    weights = probs / jnp.sum(probs, axis=1, keepdims=True)
    mixed = tokens_in.astype(jnp.float32) + jnp.sum(
        per_route.reshape(tok_count, route_count, model_width) * weights[:, :, None], axis=1
    )
    return mixed.astype(jnp.bfloat16)


def body(act_fwd, act_rev, ids_fwd, ids_rev, probs_fwd, probs_rev, w_gate, w_up, w_down):
    arrived_fwd = from_behind(act_fwd, "section", 1)
    arrived_rev = from_behind(act_rev, "section", -1)
    out_fwd = moe_layer(arrived_fwd[0], ids_fwd[0], probs_fwd[0], w_gate, w_up, w_down)
    out_rev = moe_layer(arrived_rev[0], ids_rev[0], probs_rev[0], w_gate, w_up, w_down)
    return (out_fwd[None], out_rev[None])


def solution(mesh):
    return jax.shard_map(
        body,
        mesh=mesh,
        in_specs=(
            P("section", "expert", None),
            P("section", "expert", None),
            P("section", "expert", None),
            P("section", "expert", None),
            P("section", "expert", None),
            P("section", "expert", None),
            P("section", None, "expert"),
            P("section", None, "expert"),
            P("section", "expert", None),
        ),
        out_specs=(P("section", "expert", None), P("section", "expert", None)),
        check_vma=False,
    )
```

profile of v0, /device:TPU:11, one launch (start us, length us, event | category | flops | bytes accessed | tf_op | source)
XLA Modules:
  0.0 619.1 jit_solution(8545533686680316492)
XLA Ops:
  0.6 0.0 copy-start
  0.6 1.3 collective-permute-start.1
  2.0 0.8 copy.26
  2.7 0.1 eq.155
  2.9 0.1 eq.151
  3.0 0.6 reduce-window.16
  3.6 0.2 slice_reduce_fusion
  3.9 0.1 fusion.38
  4.0 0.1 reduce_sum.118
  4.1 0.1 copy.29
  4.2 0.1 fusion.34
  4.3 20.8 %collective-permute-done.1 = bf16[1,128,4096]{2,1,0:T(8,128)(2,1)} collective-permute-done((bf16[1,128,4096]{2,1,0:T(8,128)(2,1)}, bf16[1,128,4096]{2,1,0:T(8,128)(2,1)}, u32[]{:S(2)}, u32[]{:S(2)}) %collective-permute-start.1) | collective-permute-done | bytes 1048608 | tf_op jit(solution)/shard_map/ppermute | solution.py:10
  25.1 2.2 convolution_convert_fusion.2
  27.3 3.4 broadcast_in_dim.5
  30.7 7.6 %all-to-all-start.2 = ((bf16[16,48,4096]{2,1,0:T(8,128)(2,1)}), bf16[16,48,4096]{2,1,0:T(8,128)(2,1)}, u32[]{:S(2)}, u32[]{:S(2)}) async-start(bf16[16,48,4096]{2,1,0:T(8,128)(2,1)} %bitcast.91), calls=%async_computation.2 | async-start | bytes 12582912 | tf_op jit(solution)/shard_map/all_to_all | solution.py:47
  38.2 1.2 collective-permute-start
  39.5 0.1 copy.21
  39.6 0.1 eq.140
  39.7 0.1 eq.136
  39.9 0.6 reduce-window.14
  40.5 0.2 slice_reduce_fusion.1
  40.7 0.1 fusion.39
  40.8 0.1 reduce_sum.111
  41.0 0.1 copy.24
  41.1 0.1 fusion.35
  41.1 21.8 %collective-permute-done = bf16[1,128,4096]{2,1,0:T(8,128)(2,1)} collective-permute-done((bf16[1,128,4096]{2,1,0:T(8,128)(2,1)}, bf16[1,128,4096]{2,1,0:T(8,128)(2,1)}, u32[]{:S(2)}, u32[]{:S(2)}) %collective-permute-start) | collective-permute-done | bytes 1048608 | tf_op jit(solution)/shard_map/ppermute | solution.py:10
  62.9 3.9 convolution_convert_fusion.3
  66.8 108.8 %all-to-all-done.2 = bf16[16,48,4096]{2,1,0:T(8,128)(2,1)} async-done(((bf16[16,48,4096]{2,1,0:T(8,128)(2,1)}), bf16[16,48,4096]{2,1,0:T(8,128)(2,1)}, u32[]{:S(2)}, u32[]{:S(2)}) %all-to-all-start.2) | async-done | bytes 6291488 | tf_op jit(solution)/shard_map/all_to_all | solution.py:47
  175.7 5.3 broadcast_in_dim.4
  181.0 4.9 all-to-all-start
  185.9 6.6 %fusion.6 = f32[768,384]{1,0:T(8,128)S(1)} fusion(bf16[768,4096]{1,0:T(8,128)(2,1)} %bitcast.24, bf16[1,4096,384]{2,1,0:T(8,128)(2,1)} %param.15), kind=kOutput, calls=%fused_computation.14 | convolution fusion | flops 2415919104 | bytes 10616832 | tf_op jit(solution)/shard_map/dot_general | solution.py:16
  192.5 6.3 %fusion.20 = bf16[768,384]{1,0:T(8,128)(2,1)S(1)} fusion(bf16[768,4096]{1,0:T(8,128)(2,1)} %bitcast.24, bf16[1,4096,384]{2,1,0:T(8,128)(2,1)S(1)} %copy-done.5, f32[768,384]{1,0:T(8,128)S(1)} %fusion.6), kind=kOutput, calls=%fused_computation.26 | convolution fusion | flops 2417688576 | bytes 11206656 | tf_op jit(solution)/shard_map/dot_general | solution.py:17
  198.8 5.3 convolution_convert_fusion
  204.1 119.2 %all-to-all-done = bf16[16,48,4096]{2,1,0:T(8,128)(2,1)} async-done(((bf16[16,48,4096]{2,1,0:T(8,128)(2,1)}), bf16[16,48,4096]{2,1,0:T(8,128)(2,1)}, u32[]{:S(2)}, u32[]{:S(2)}) %all-to-all-start) | async-done | bytes 6291488 | tf_op jit(solution)/shard_map/all_to_all | solution.py:47
  323.3 4.9 all-to-all-start.3
  328.2 6.6 %fusion.8 = f32[768,384]{1,0:T(8,128)S(1)} fusion(bf16[768,4096]{1,0:T(8,128)(2,1)} %bitcast.7, bf16[1,4096,384]{2,1,0:T(8,128)(2,1)} %param.15), kind=kOutput, calls=%fused_computation.16 | convolution fusion | flops 2415919104 | bytes 10616832 | tf_op jit(solution)/shard_map/dot_general | solution.py:16
  334.8 6.3 %fusion.23 = bf16[768,384]{1,0:T(8,128)(2,1)S(1)} fusion(bf16[768,4096]{1,0:T(8,128)(2,1)} %bitcast.7, bf16[1,4096,384]{2,1,0:T(8,128)(2,1)S(1)} %copy-done.6, f32[768,384]{1,0:T(8,128)S(1)} %fusion.8), kind=kOutput, calls=%fused_computation.27 | convolution fusion | flops 2417688576 | bytes 11206656 | tf_op jit(solution)/shard_map/dot_general | solution.py:17
  341.1 5.4 convolution_convert_fusion.1
  346.5 119.1 %all-to-all-done.3 = bf16[16,48,4096]{2,1,0:T(8,128)(2,1)} async-done(((bf16[16,48,4096]{2,1,0:T(8,128)(2,1)}), bf16[16,48,4096]{2,1,0:T(8,128)(2,1)}, u32[]{:S(2)}, u32[]{:S(2)}) %all-to-all-start.3) | async-done | bytes 6291488 | tf_op jit(solution)/shard_map/all_to_all | solution.py:52
  465.6 5.0 all-to-all-start.1
  470.7 4.6 bitcast_reduce_fusion
  475.3 2.8 fusion.13
  478.1 129.9 %all-to-all-done.1 = bf16[16,48,4096]{2,1,0:T(8,128)(2,1)} async-done(((bf16[16,48,4096]{2,1,0:T(8,128)(2,1)}), bf16[16,48,4096]{2,1,0:T(8,128)(2,1)}, u32[]{:S(2)}, u32[]{:S(2)}) %all-to-all-start.1) | async-done | bytes 6291488 | tf_op jit(solution)/shard_map/all_to_all | solution.py:52
  608.0 4.6 bitcast_reduce_fusion.1
  612.6 1.5 fusion.12
  614.1 0.1 copy-done.1
  614.2 2.4 fusion.10
  616.6 2.4 fusion.11
  (24 shorter events, 0.2 us)
Async XLA Ops:
  0.6 198.1 %copy-start = (bf16[1,384,4096]{2,1,0:T(8,128)(2,1)S(1)}, bf16[1,384,4096]{2,1,0:T(8,128)(2,1)}, u32[]{:S(2)}) copy-start(bf16[1,384,4096]{2,1,0:T(8,128)(2,1)} %param.17) | copy-start | bytes 9437188
  0.6 24.4 %collective-permute-start.1 = (bf16[1,128,4096]{2,1,0:T(8,128)(2,1)}, bf16[1,128,4096]{2,1,0:T(8,128)(2,1)}, u32[]{:S(2)}, u32[]{:S(2)}) collective-permute-start(bf16[1,128,4096]{2,1,0:T(8,128)(2,1)} %param.10), channel_id=1, source_target_pairs={{16,0},{0,16},{17,1},{1,17},{18,2},{2,18},{19,3},{3,19},{20,4},{4,... | collective-permute-start | bytes 3145736 | tf_op jit(solution)/shard_map/ppermute | solution.py:10
  30.7 8.8 %copy-start.4 = (s32[1,128,2]{1,2,0:T(2,128)S(1)}, s32[1,128,2]{1,2,0:T(2,128)}, u32[]{:S(2)}) copy-start(s32[1,128,2]{1,2,0:T(2,128)} %param.11) | copy-start | bytes 3076
  30.7 145.0 %all-to-all-start.2 = ((bf16[16,48,4096]{2,1,0:T(8,128)(2,1)}), bf16[16,48,4096]{2,1,0:T(8,128)(2,1)}, u32[]{:S(2)}, u32[]{:S(2)}) async-start(bf16[16,48,4096]{2,1,0:T(8,128)(2,1)} %bitcast.91), calls=%async_computation.2 | async-start | bytes 12582912 | tf_op jit(solution)/shard_map/all_to_all | solution.py:47
  38.2 24.7 %collective-permute-start = (bf16[1,128,4096]{2,1,0:T(8,128)(2,1)}, bf16[1,128,4096]{2,1,0:T(8,128)(2,1)}, u32[]{:S(2)}, u32[]{:S(2)}) collective-permute-start(bf16[1,128,4096]{2,1,0:T(8,128)(2,1)} %param.9), channel_id=1, source_target_pairs={{16,0},{0,16},{17,1},{1,17},{18,2},{2,18},{19,3},{3,19},{20,4},{4,... | collective-permute-start | bytes 3145736 | tf_op jit(solution)/shard_map/ppermute | solution.py:10
  181.0 142.3 %all-to-all-start = ((bf16[16,48,4096]{2,1,0:T(8,128)(2,1)}), bf16[16,48,4096]{2,1,0:T(8,128)(2,1)}, u32[]{:S(2)}, u32[]{:S(2)}) async-start(bf16[16,48,4096]{2,1,0:T(8,128)(2,1)} %bitcast.92), calls=%async_computation | async-start | bytes 12582912 | tf_op jit(solution)/shard_map/all_to_all | solution.py:47
  185.9 6.6 %copy-start.5 = (bf16[1,4096,384]{2,1,0:T(8,128)(2,1)S(1)}, bf16[1,4096,384]{2,1,0:T(8,128)(2,1)}, u32[]{:S(2)}) copy-start(bf16[1,4096,384]{2,1,0:T(8,128)(2,1)} %param.16) | copy-start | bytes 9437188
  323.3 142.3 %all-to-all-start.3 = ((bf16[16,48,4096]{2,1,0:T(8,128)(2,1)}), bf16[16,48,4096]{2,1,0:T(8,128)(2,1)}, u32[]{:S(2)}, u32[]{:S(2)}) async-start(bf16[16,48,4096]{2,1,0:T(8,128)(2,1)} %bitcast.96), calls=%async_computation.3 | async-start | bytes 12582912 | tf_op jit(solution)/shard_map/all_to_all | solution.py:52
  328.2 6.6 %copy-start.6 = (bf16[1,4096,384]{2,1,0:T(8,128)(2,1)S(1)}, bf16[1,4096,384]{2,1,0:T(8,128)(2,1)}, u32[]{:S(2)}) copy-start(bf16[1,4096,384]{2,1,0:T(8,128)(2,1)} %param.16) | copy-start | bytes 9437188
  465.6 5.0 copy-start.2
  465.6 5.1 copy-start.3
  465.6 142.4 %all-to-all-start.1 = ((bf16[16,48,4096]{2,1,0:T(8,128)(2,1)}), bf16[16,48,4096]{2,1,0:T(8,128)(2,1)}, u32[]{:S(2)}, u32[]{:S(2)}) async-start(bf16[16,48,4096]{2,1,0:T(8,128)(2,1)} %bitcast.95), calls=%async_computation.1 | async-start | bytes 12582912 | tf_op jit(solution)/shard_map/all_to_all | solution.py:52
  612.6 1.6 copy-start.1
where the time goes:
time: 620 us; the launch traced here: 619 us
  waiting for transfers between devices  520 us (84%)
  matrix products  46.9 us (8%)
  starting transfers between devices  25 us (4%)
  other arithmetic  15.6 us (3%)
  local copies, waits for them, and re-layouts  11.1 us (2%)
    all_to_all x2, waiting for transfers between devices, moe_layer(): lax.all_to_all(partial_value, 'expert', split_axis=0, concat_axis=0, tile...  249 us
    all_to_all x2, waiting for transfers between devices, moe_layer(): lax.all_to_all(outgoing_all, 'expert', split_axis=0, concat_axis=0, tiled...  228 us
    ppermute x2, waiting for transfers between devices, from_behind(): return lax.ppermute(block, axis, route)  42.6 us
    dot_general x2, matrix products, expert_rows(): gate_pre = jnp.dot(flat_rows, w_gate[0], preferred_element_type=jnp.float32)  13.2 us
    dot_general x2, matrix products, expert_rows(): up_pre = jnp.dot(flat_rows, w_up[0], preferred_element_type=jnp.float32)  12.6 us
    all_to_all x2, starting transfers between devices, moe_layer(): lax.all_to_all(outgoing_all, 'expert', split_axis=0, concat_axis=0, tiled...  12.5 us
  transfers between devices with their start and end apart: 6, of which 6 were waited for; matrix products, arithmetic and copies ran while one was open for 8% of the time, Pallas kernels for 0%

commit v1 on v0

v1 whole, which is shorter than its diff:
```python
import jax
import jax.numpy as jnp
from jax import lax
from jax.sharding import PartitionSpec as P


def from_behind(block, axis, distance):
    devices = range(lax.axis_size(axis))
    route = [((i - distance) % len(devices), i) for i in devices]
    return lax.ppermute(block, axis, route)


def from_core(block):
    devices = range(lax.axis_size("expert"))
    return lax.ppermute(block, "expert", [(i, i + 1 - 2 * (i % 2)) for i in devices])


def half_expert(rows, w_gate, w_up, w_down):
    gate_pre = jnp.dot(rows, w_gate, preferred_element_type=jnp.float32)
    up_pre = jnp.dot(rows, w_up, preferred_element_type=jnp.float32)
    hidden = (jax.nn.silu(gate_pre) * up_pre).astype(jnp.bfloat16)
    return jnp.dot(hidden, w_down, preferred_element_type=jnp.float32).astype(jnp.bfloat16)


def moe_layer(tokens_in, route_ids, probs, weights_here, weights_there):
    tok_count, route_count = route_ids.shape
    model_width = tokens_in.shape[1]
    device_count = lax.axis_size("expert")
    expert_count = device_count // 2
    groups = [list(range(0, device_count, 2)), list(range(1, device_count, 2))]
    slot_count = 2 * (3 * tok_count * route_count // (4 * expert_count))
    flat_ids = route_ids.reshape(-1)
    one_hot = (flat_ids[:, None] == jnp.arange(expert_count, dtype=jnp.int32)[None, :]).astype(
        jnp.int32
    )
    rank_in = jnp.sum((jnp.cumsum(one_hot, axis=0) - 1) * one_hot, axis=1)
    slot_of = flat_ids * slot_count + rank_in
    slot_range = jnp.arange(expert_count * slot_count, dtype=jnp.int32)
    pick_rows = (slot_range[:, None] == slot_of[None, :]).astype(jnp.bfloat16)
    pick_tokens = jnp.sum(
        pick_rows.reshape(expert_count * slot_count, tok_count, route_count), axis=2
    )
    outgoing = jnp.dot(pick_tokens, tokens_in, preferred_element_type=jnp.float32).astype(
        jnp.bfloat16
    )
    received = lax.all_to_all(
        outgoing.reshape(expert_count, slot_count, model_width),
        "expert", split_axis=0, concat_axis=0, tiled=True, axis_index_groups=groups,
    ).reshape(-1, model_width)
    here = half_expert(received, *weights_here)
    there = half_expert(received, *weights_there)
    expert_sum = (here.astype(jnp.float32) + there.astype(jnp.float32)).astype(jnp.bfloat16)
    expert_out = lax.all_to_all(
        expert_sum.reshape(expert_count, slot_count, model_width),
        "expert", split_axis=0, concat_axis=0, tiled=True, axis_index_groups=groups,
    ).reshape(-1, model_width)
    route_pick = (slot_of[:, None] == slot_range[None, :]).astype(jnp.bfloat16)
    per_route = jnp.dot(route_pick, expert_out, preferred_element_type=jnp.float32)
    weights = probs / jnp.sum(probs, axis=1, keepdims=True)
    mixed = tokens_in.astype(jnp.float32) + jnp.sum(
        per_route.reshape(tok_count, route_count, model_width) * weights[:, :, None], axis=1
    )
    return mixed.astype(jnp.bfloat16)


def body(act_fwd, act_rev, ids_fwd, ids_rev, probs_fwd, probs_rev, w_gate, w_up, w_down):
    here = (w_gate[0], w_up[0], w_down[0])
    arrived_fwd = from_behind(act_fwd, "section", 1)
    there = tuple(from_core(w) for w in here)
    arrived_rev = from_behind(act_rev, "section", -1)
    out_fwd = moe_layer(arrived_fwd[0], ids_fwd[0], probs_fwd[0], here, there)
    out_rev = moe_layer(arrived_rev[0], ids_rev[0], probs_rev[0], here, there)
    return (out_fwd[None], out_rev[None])


def solution(mesh):
    return jax.shard_map(
        body,
        mesh=mesh,
        in_specs=(
            P("section", "expert", None),
            P("section", "expert", None),
            P("section", "expert", None),
            P("section", "expert", None),
            P("section", "expert", None),
            P("section", "expert", None),
            P("section", None, "expert"),
            P("section", None, "expert"),
            P("section", "expert", None),
        ),
        out_specs=(P("section", "expert", None), P("section", "expert", None)),
        check_vma=False,
    )
```

time: 620 us -> 337 us (0.54)
  the two profiles are of different devices: /device:TPU:11 before, /device:TPU:0 now
where the time goes in v1:
time: 337 us; the launch traced here: 336 us
  waiting for transfers between devices  234 us (69%)
  matrix products  68.1 us (20%)
  starting transfers between devices  25.1 us (7%)
  other arithmetic  4.13 us (1%)
  local copies, waits for them, and re-layouts  3.97 us (1%)
    all_to_all x2, waiting for transfers between devices, moe_layer(): lax.all_to_all(expert_sum.reshape(expert_count, slot_count, model_width),...  108 us
    all_to_all x2, waiting for transfers between devices, moe_layer(): lax.all_to_all(outgoing.reshape(expert_count, slot_count, model_width), '...  79.8 us
    ppermute x2, waiting for transfers between devices, from_behind(): return lax.ppermute(block, axis, route)  41.6 us
    dot_general x4, matrix products, half_expert(): jnp.dot(hidden, w_down, preferred_element_type=jnp.float32)  37.6 us
    dot_general x4, matrix products, half_expert(): gate_pre = jnp.dot(rows, w_gate, preferred_element_type=jnp.float32)  16.8 us
    all_to_all x2, starting transfers between devices, moe_layer(): lax.all_to_all(outgoing.reshape(expert_count, slot_count, model_width), '...  10.6 us
    all_to_all x2, starting transfers between devices, moe_layer(): lax.all_to_all(expert_sum.reshape(expert_count, slot_count, model_width),...  9.19 us
    dot_general x2, matrix products, moe_layer(): jnp.dot(route_pick, expert_out, preferred_element_type=jnp.float32)  8.52 us
  transfers between devices with their start and end apart: 9, of which 7 were waited for; matrix products, arithmetic and copies ran while one was open for 20% of the time, Pallas kernels for 0%

profile of v1, /device:TPU:0, one launch (start us, length us, event | category | flops | bytes accessed | tf_op | source)
XLA Modules:
  0.0 336.0 jit_solution(14858919385479702851)
XLA Ops:
  0.6 3.0 collective-permute-start.4
  3.7 0.8 copy.26
  4.4 0.1 eq.155
  4.6 0.1 eq.151
  4.7 0.6 reduce-window.16
  5.3 0.2 slice_reduce_fusion
  5.6 0.1 fusion.32
  5.7 0.1 reduce_sum.93
  5.8 0.1 copy.29
  5.9 0.1 fusion.28
  6.0 21.0 %collective-permute-done.4 = bf16[1,128,4096]{2,1,0:T(8,128)(2,1)S(1)} collective-permute-done((bf16[1,128,4096]{2,1,0:T(8,128)(2,1)}, bf16[1,128,4096]{2,1,0:T(8,128)(2,1)S(1)}, u32[]{:S(2)}, u32[]{:S(2)}) %collective-permute-start.4) | collective-permute-done | bytes 1048608 | tf_op jit(solution)/shard_map/ppermute | solution.py:10
  27.0 2.6 convolution_convert_fusion.4
  29.7 6.2 %all-to-all-start.2 = ((bf16[8,48,4096]{2,1,0:T(8,128)(2,1)}), bf16[8,48,4096]{2,1,0:T(8,128)(2,1)}, u32[]{:S(2)}, u32[]{:S(2)}) async-start(bf16[8,48,4096]{2,1,0:T(8,128)(2,1)} %bitcast.20), calls=%async_computation.2 | async-start | bytes 6291456 | tf_op jit(solution)/shard_map/all_to_all | solution.py:46
  35.8 1.6 collective-permute-start
  37.4 0.1 copy.21
  37.5 0.1 eq.140
  37.7 0.1 eq.136
  37.8 0.6 reduce-window.14
  38.4 0.2 slice_reduce_fusion.1
  38.7 0.1 fusion.33
  38.8 0.1 reduce_sum.87
  39.0 0.1 fusion.29
  39.1 20.6 %collective-permute-done = bf16[1,128,4096]{2,1,0:T(8,128)(2,1)S(1)} collective-permute-done((bf16[1,128,4096]{2,1,0:T(8,128)(2,1)S(1)}, bf16[1,128,4096]{2,1,0:T(8,128)(2,1)S(1)}, u32[]{:S(2)}, u32[]{:S(2)}) %collective-permute-start) | collective-permute-done | bytes 1048608 | tf_op jit(solution)/shard_map/ppermute | solution.py:10
  59.6 2.6 convolution_convert_fusion.5
  62.3 43.5 %all-to-all-done.2 = bf16[8,48,4096]{2,1,0:T(8,128)(2,1)} async-done(((bf16[8,48,4096]{2,1,0:T(8,128)(2,1)}), bf16[8,48,4096]{2,1,0:T(8,128)(2,1)}, u32[]{:S(2)}, u32[]{:S(2)}) %all-to-all-start.2) | async-done | bytes 3145760 | tf_op jit(solution)/shard_map/all_to_all | solution.py:46
  105.8 4.4 %all-to-all-start = ((bf16[8,48,4096]{2,1,0:T(8,128)(2,1)}), bf16[8,48,4096]{2,1,0:T(8,128)(2,1)}, u32[]{:S(2)}, u32[]{:S(2)}) async-start(bf16[8,48,4096]{2,1,0:T(8,128)(2,1)} %bitcast.5), calls=%async_computation | async-start | bytes 6291456 | tf_op jit(solution)/shard_map/all_to_all | solution.py:46
  110.2 0.1 collective-permute-start.1
  110.3 0.5 collective-permute-start.2
  110.8 0.1 collective-permute-start.3
  110.9 4.6 %fusion.42 = f32[384,384]{1,0:T(8,128)S(1)} fusion(bf16[384,4096]{1,0:T(8,128)(2,1)} %bitcast.21, bf16[1,4096,384]{2,1,0:T(8,128)(2,1)} %param.15), kind=kOutput, calls=%fused_computation.70 | convolution fusion | flops 1207959552 | bytes 6881280 | tf_op jit(solution)/shard_map/dot_general | solution.py:19
  115.5 4.3 %collective-permute-done.1 = bf16[4096,384]{1,0:T(8,128)(2,1)S(1)} collective-permute-done((bf16[4096,384]{1,0:T(8,128)(2,1)}, bf16[4096,384]{1,0:T(8,128)(2,1)S(1)}, u32[]{:S(2)}, u32[]{:S(2)}) %collective-permute-start.1) | collective-permute-done | bytes 3145760 | tf_op jit(solution)/shard_map/ppermute | solution.py:15
  119.8 1.7 copy-done.4
  121.5 3.7 %fusion.55 = f32[384,384]{1,0:T(8,128)S(1)} fusion(bf16[384,4096]{1,0:T(8,128)(2,1)} %bitcast.21, bf16[4096,384]{1,0:T(8,128)(2,1)S(1)} %collective-permute-done.1), kind=kOutput, calls=%fused_computation.81 | convolution fusion | flops 1207959552 | bytes 6881280 | tf_op jit(solution)/shard_map/dot_general | solution.py:19
  125.2 8.9 %convolution_convert_fusion.1 = bf16[384,4096]{1,0:T(8,128)(2,1)} fusion(bf16[384,4096]{1,0:T(8,128)(2,1)} %bitcast.21, f32[384,384]{1,0:T(8,128)S(1)} %fusion.42, bf16[1,384,4096]{2,1,0:T(8,128)(2,1)} %param.17, bf16[1,4096,384]{2,1,0:T(8,128)(2,1)} %param.16), kind=kOutput, calls=%fused_computation.3 | convolution fusion | flops 2418376704 | bytes 13172736 | tf_op jit(solution)/shard_map/dot_general | solution.py:22
  134.1 9.9 %add_convert_fusion = bf16[384,4096]{1,0:T(8,128)(2,1)} fusion(bf16[384,4096]{1,0:T(8,128)(2,1)} %convolution_convert_fusion.1, bf16[384,4096]{1,0:T(8,128)(2,1)} %collective-permute-done.3, f32[384,384]{1,0:T(8,128)S(1)} %fusion.55, bf16[384,4096]{1,0:T(8,128)(2,1)} %bitcast.21, bf16[4096,384]{1,0:T(8,128)(2,1)} %collective-permute-done.2), kind=kOutput, calls=%fused_computation | convolution fusion | flops 2424668160 | bytes 16318464 | tf_op jit(solution)/shard_map/dot_general | solution.py:22
  144.1 36.4 %all-to-all-done = bf16[8,48,4096]{2,1,0:T(8,128)(2,1)} async-done(((bf16[8,48,4096]{2,1,0:T(8,128)(2,1)}), bf16[8,48,4096]{2,1,0:T(8,128)(2,1)}, u32[]{:S(2)}, u32[]{:S(2)}) %all-to-all-start) | async-done | bytes 3145760 | tf_op jit(solution)/shard_map/all_to_all | solution.py:46
  180.4 4.6 %all-to-all-start.3 = ((bf16[8,48,4096]{2,1,0:T(8,128)(2,1)}), bf16[8,48,4096]{2,1,0:T(8,128)(2,1)}, u32[]{:S(2)}, u32[]{:S(2)}) async-start(bf16[8,48,4096]{2,1,0:T(8,128)(2,1)} %bitcast.88), calls=%async_computation.3 | async-start | bytes 6291456 | tf_op jit(solution)/shard_map/all_to_all | solution.py:53
  185.1 4.8 %fusion.44 = f32[384,384]{1,0:T(8,128)S(1)} fusion(bf16[384,4096]{1,0:T(8,128)(2,1)} %bitcast.6, bf16[1,4096,384]{2,1,0:T(8,128)(2,1)} %param.15), kind=kOutput, calls=%fused_computation.72 | convolution fusion | flops 1207959552 | bytes 6881280 | tf_op jit(solution)/shard_map/dot_general | solution.py:19
  189.8 3.7 %fusion.54 = f32[384,384]{1,0:T(8,128)S(1)} fusion(bf16[384,4096]{1,0:T(8,128)(2,1)} %bitcast.6, bf16[4096,384]{1,0:T(8,128)(2,1)S(1)} %copy-done.5), kind=kOutput, calls=%fused_computation.80 | convolution fusion | flops 1207959552 | bytes 6881280 | tf_op jit(solution)/shard_map/dot_general | solution.py:19
  193.5 8.9 %convolution_convert_fusion.3 = bf16[384,4096]{1,0:T(8,128)(2,1)} fusion(bf16[384,4096]{1,0:T(8,128)(2,1)} %bitcast.6, f32[384,384]{1,0:T(8,128)S(1)} %fusion.44, bf16[1,384,4096]{2,1,0:T(8,128)(2,1)} %param.17, bf16[1,4096,384]{2,1,0:T(8,128)(2,1)} %param.16), kind=kOutput, calls=%fused_computation.5 | convolution fusion | flops 2418376704 | bytes 13172736 | tf_op jit(solution)/shard_map/dot_general | solution.py:22
  202.5 9.8 %add_convert_fusion.1 = bf16[384,4096]{1,0:T(8,128)(2,1)} fusion(bf16[384,4096]{1,0:T(8,128)(2,1)} %convolution_convert_fusion.3, bf16[384,4096]{1,0:T(8,128)(2,1)} %collective-permute-done.3, f32[384,384]{1,0:T(8,128)S(1)} %fusion.54, bf16[384,4096]{1,0:T(8,128)(2,1)} %bitcast.6, bf16[4096,384]{1,0:T(8,128)(2,1)} %collective-permute-done.2), kind=kOutput, calls=%fused_computation.1 | convolution fusion | flops 2424668160 | bytes 16318464 | tf_op jit(solution)/shard_map/dot_general | solution.py:22
  212.3 42.9 %all-to-all-done.3 = bf16[8,48,4096]{2,1,0:T(8,128)(2,1)} async-done(((bf16[8,48,4096]{2,1,0:T(8,128)(2,1)}), bf16[8,48,4096]{2,1,0:T(8,128)(2,1)}, u32[]{:S(2)}, u32[]{:S(2)}) %all-to-all-start.3) | async-done | bytes 3145760 | tf_op jit(solution)/shard_map/all_to_all | solution.py:53
  255.1 4.6 %all-to-all-start.1 = ((bf16[8,48,4096]{2,1,0:T(8,128)(2,1)}), bf16[8,48,4096]{2,1,0:T(8,128)(2,1)}, u32[]{:S(2)}, u32[]{:S(2)}) async-start(bf16[8,48,4096]{2,1,0:T(8,128)(2,1)} %bitcast.87), calls=%async_computation.1 | async-start | bytes 6291456 | tf_op jit(solution)/shard_map/all_to_all | solution.py:53
  259.8 4.8 %fusion.3 = f32[128,4096]{1,0:T(8,128)} fusion(f32[128,2]{0,1:T(2,128)S(1)} %bitcast_divide_fusion, bf16[384,4096,1]{1,0,2:T(8,128)(2,1)} %bitcast.24, s32[128,2]{0,1:T(2,128)S(1)} %copy.29), kind=kOutput, calls=%fused_computation.15 | convolution fusion | flops 806977536 | bytes 5244928 | tf_op jit(solution)/shard_map/dot_general | solution.py:58
  264.6 65.2 %all-to-all-done.1 = bf16[8,48,4096]{2,1,0:T(8,128)(2,1)} async-done(((bf16[8,48,4096]{2,1,0:T(8,128)(2,1)}), bf16[8,48,4096]{2,1,0:T(8,128)(2,1)}, u32[]{:S(2)}, u32[]{:S(2)}) %all-to-all-start.1) | async-done | bytes 3145760 | tf_op jit(solution)/shard_map/all_to_all | solution.py:53
  329.8 3.7 %fusion.2 = f32[128,4096]{1,0:T(8,128)S(1)} fusion(f32[128,2]{0,1:T(2,128)S(1)} %bitcast_divide_fusion.1, bf16[384,4096,1]{1,0,2:T(8,128)(2,1)} %bitcast.12, s32[128,2]{0,1:T(2,128)S(1)} %copy.24), kind=kOutput, calls=%fused_computation.14 | convolution fusion | flops 806977536 | bytes 5244928 | tf_op jit(solution)/shard_map/dot_general | solution.py:58
  333.5 1.2 fusion
  334.7 1.3 fusion.1
  (28 shorter events, 0.3 us)
Async XLA Ops:
  0.6 26.4 %collective-permute-start.4 = (bf16[1,128,4096]{2,1,0:T(8,128)(2,1)}, bf16[1,128,4096]{2,1,0:T(8,128)(2,1)S(1)}, u32[]{:S(2)}, u32[]{:S(2)}) collective-permute-start(bf16[1,128,4096]{2,1,0:T(8,128)(2,1)} %param.10), channel_id=1, source_target_pairs={{16,0},{0,16},{17,1},{1,17},{18,2},{2,18},{19,3},{3,19},{20,4},{4,... | collective-permute-start | bytes 3145736 | tf_op jit(solution)/shard_map/ppermute | solution.py:10
  29.7 6.2 %copy-start.6 = (bf16[1,128,4096]{2,1,0:T(8,128)(2,1)S(1)}, bf16[1,128,4096]{2,1,0:T(8,128)(2,1)}, u32[]{:S(2)}) copy-start(bf16[1,128,4096]{2,1,0:T(8,128)(2,1)} %param.9) | copy-start | bytes 3145732
  29.7 7.8 %copy-start.3 = (s32[1,128,2]{1,2,0:T(2,128)S(1)}, s32[1,128,2]{1,2,0:T(2,128)}, u32[]{:S(2)}) copy-start(s32[1,128,2]{1,2,0:T(2,128)} %param.11) | copy-start | bytes 3076
  29.7 76.1 %all-to-all-start.2 = ((bf16[8,48,4096]{2,1,0:T(8,128)(2,1)}), bf16[8,48,4096]{2,1,0:T(8,128)(2,1)}, u32[]{:S(2)}, u32[]{:S(2)}) async-start(bf16[8,48,4096]{2,1,0:T(8,128)(2,1)} %bitcast.20), calls=%async_computation.2 | async-start | bytes 6291456 | tf_op jit(solution)/shard_map/all_to_all | solution.py:46
  35.8 23.8 %collective-permute-start = (bf16[1,128,4096]{2,1,0:T(8,128)(2,1)S(1)}, bf16[1,128,4096]{2,1,0:T(8,128)(2,1)S(1)}, u32[]{:S(2)}, u32[]{:S(2)}) collective-permute-start(bf16[1,128,4096]{2,1,0:T(8,128)(2,1)S(1)} %copy-done.6), channel_id=1, source_target_pairs={{16,0},{0,16},{17,1},{1,17},{18,2},{2,18},{19,3},{3,19},{20,4},{4,... | collective-permute-start | bytes 3145736 | tf_op jit(solution)/shard_map/ppermute | solution.py:10
  105.8 74.7 %all-to-all-start = ((bf16[8,48,4096]{2,1,0:T(8,128)(2,1)}), bf16[8,48,4096]{2,1,0:T(8,128)(2,1)}, u32[]{:S(2)}, u32[]{:S(2)}) async-start(bf16[8,48,4096]{2,1,0:T(8,128)(2,1)} %bitcast.5), calls=%async_computation | async-start | bytes 6291456 | tf_op jit(solution)/shard_map/all_to_all | solution.py:46
  110.2 9.6 %collective-permute-start.1 = (bf16[4096,384]{1,0:T(8,128)(2,1)}, bf16[4096,384]{1,0:T(8,128)(2,1)S(1)}, u32[]{:S(2)}, u32[]{:S(2)}) collective-permute-start(bf16[4096,384]{1,0:T(8,128)(2,1)} %bitcast.89), channel_id=1, source_target_pairs={{0,1},{1,0},{2,3},{3,2},{4,5},{5,4},{6,7},{7,6},{8,9},{9,8},{10,11... | collective-permute-start | bytes 9437192 | tf_op jit(solution)/shard_map/ppermute | solution.py:15
  110.3 23.8 %collective-permute-start.2 = (bf16[4096,384]{1,0:T(8,128)(2,1)}, bf16[4096,384]{1,0:T(8,128)(2,1)}, u32[]{:S(2)}, u32[]{:S(2)}) collective-permute-start(bf16[4096,384]{1,0:T(8,128)(2,1)} %bitcast.91), channel_id=1, source_target_pairs={{0,1},{1,0},{2,3},{3,2},{4,5},{5,4},{6,7},{7,6},{8,9},{9,8},{10,11... | collective-permute-start | bytes 9437192 | tf_op jit(solution)/shard_map/ppermute | solution.py:15
  110.8 23.3 %collective-permute-start.3 = (bf16[384,4096]{1,0:T(8,128)(2,1)}, bf16[384,4096]{1,0:T(8,128)(2,1)}, u32[]{:S(2)}, u32[]{:S(2)}) collective-permute-start(bf16[384,4096]{1,0:T(8,128)(2,1)} %bitcast.90), channel_id=1, source_target_pairs={{0,1},{1,0},{2,3},{3,2},{4,5},{5,4},{6,7},{7,6},{8,9},{9,8},{10,11... | collective-permute-start | bytes 9437192 | tf_op jit(solution)/shard_map/ppermute | solution.py:15
  119.8 1.7 copy-start.4
  180.4 74.7 %all-to-all-start.3 = ((bf16[8,48,4096]{2,1,0:T(8,128)(2,1)}), bf16[8,48,4096]{2,1,0:T(8,128)(2,1)}, u32[]{:S(2)}, u32[]{:S(2)}) async-start(bf16[8,48,4096]{2,1,0:T(8,128)(2,1)} %bitcast.88), calls=%async_computation.3 | async-start | bytes 6291456 | tf_op jit(solution)/shard_map/all_to_all | solution.py:53
  185.1 4.8 %copy-start.5 = (bf16[4096,384]{1,0:T(8,128)(2,1)S(1)}, bf16[4096,384]{1,0:T(8,128)(2,1)}, u32[]{:S(2)}) copy-start(bf16[4096,384]{1,0:T(8,128)(2,1)} %copy-done.4) | copy-start | bytes 9437188
  255.1 4.6 %copy-start.1 = (f32[1,128,2]{1,2,0:T(2,128)S(1)}, f32[1,128,2]{1,2,0:T(2,128)}, u32[]{:S(2)}) copy-start(f32[1,128,2]{1,2,0:T(2,128)} %param.14) | copy-start | bytes 3076
  255.1 4.6 %copy-start.2 = (f32[1,128,2]{1,2,0:T(2,128)S(1)}, f32[1,128,2]{1,2,0:T(2,128)}, u32[]{:S(2)}) copy-start(f32[1,128,2]{1,2,0:T(2,128)} %param.13) | copy-start | bytes 3076
  255.1 74.7 %all-to-all-start.1 = ((bf16[8,48,4096]{2,1,0:T(8,128)(2,1)}), bf16[8,48,4096]{2,1,0:T(8,128)(2,1)}, u32[]{:S(2)}, u32[]{:S(2)}) async-start(bf16[8,48,4096]{2,1,0:T(8,128)(2,1)} %bitcast.87), calls=%async_computation.1 | async-start | bytes 6291456 | tf_op jit(solution)/shard_map/all_to_all | solution.py:53
  329.8 3.7 %copy-start = (f32[128,4096]{1,0:T(8,128)S(1)}, f32[128,4096]{1,0:T(8,128)}, u32[]{:S(2)}) copy-start(f32[128,4096]{1,0:T(8,128)} %fusion.3) | copy-start | bytes 6291460

commit v2 on v1

v2 whole, which is shorter than its diff:
```python
import functools

import jax
import jax.numpy as jnp
from jax import lax
from jax.experimental import pallas as pl
from jax.experimental.pallas import tpu as pltpu
from jax.sharding import PartitionSpec as P

MESH = pl.DeviceIdType.MESH
F32 = jnp.float32
BF16 = jnp.bfloat16


def kernel(
    sections, nh, slots, width,
    act_f, act_r, meta_here, w_gate, w_up, w_down,
    out_f, out_r,
    wg, wu, wd, meta_there, arrived, raw, outgoing, received, returned, part, pick, comb,
    acc_g, acc_u, hidden,
    w_local, w_send, w_recv, meta_send, meta_recv, relay_send, relay_recv, raw_send, raw_recv,
    disp_send, disp_recv, ret_send, ret_recv, part_send, part_recv,
):
    half_units = w_gate.shape[-1]
    tokens = arrived.shape[2]
    section = lax.axis_index("section")
    me = lax.axis_index("expert")
    core = lax.rem(me, 2)
    chip = me // 2
    half = chip // nh
    loc = lax.rem(chip, nh)

    def in_half(offset):
        return (section, (half * nh + lax.rem(loc + offset + nh, nh)) * 2 + core)

    partner = (section, lax.rem(chip + nh, 2 * nh) * 2 + core)
    other_core = (section, chip * 2 + 1 - core)
    after = (lax.rem(section + 1, sections), me)
    before = (lax.rem(section + sections - 1, sections), me)
    acts, outs, ways = (act_f, act_r), (out_f, out_r), (after, before)

    def columns(c):
        return pl.ds(pl.multiple_of(c * width, width), width)

    def remote(src, dst, send, recv, device):
        return pltpu.make_async_remote_copy(
            src_ref=src, dst_ref=dst, send_sem=send, recv_sem=recv,
            device_id=device, device_id_type=MESH,
        )

    def relay(st, c):
        return remote(acts[st].at[0, :, columns(c)], arrived.at[st, c],
                      relay_send.at[st, c], relay_recv.at[st, c], ways[st])

    def to_proxy(st, c):
        return remote(arrived.at[st, c], raw.at[st, c],
                      raw_send.at[st, c], raw_recv.at[st, c], partner)

    def dispatch(st, p, c, k):
        return remote(outgoing.at[st, p, c, k], received.at[st, c, k, pl.ds(p * slots, slots)],
                      disp_send.at[st, p, c, k], disp_recv.at[st, p, c, k], in_half(k))

    def give_back(st, p, c, k):
        return remote(received.at[st, c, k, pl.ds(p * slots, slots)], returned.at[st, p, c, k],
                      ret_send.at[st, p, c, k], ret_recv.at[st, p, c, k], in_half(-k))

    def from_proxy(st, c):
        return remote(raw.at[st, c], part.at[st, c],
                      part_send.at[st, c], part_recv.at[st, c], partner)

    meta_copy = remote(meta_here, meta_there, meta_send, meta_recv, partner)

    barrier = pltpu.get_barrier_semaphore()
    greeted = [after, before, partner, other_core] + [in_half(k) for k in range(1, nh)]
    for device in greeted:
        pl.semaphore_signal(barrier, inc=1, device_id=device, device_id_type=MESH)
    pl.semaphore_wait(barrier, len(greeted))

    meta_copy.start()

    @pl.loop(0, nh)
    def _(c):
        relay(0, c).start()

    here, there = pl.ds(0, half_units), pl.ds(half_units, half_units)
    places = ((w_gate, wg.at[:, here], wg.at[:, there]), (w_up, wu.at[:, here], wu.at[:, there]),
              (w_down, wd.at[here, :], wd.at[there, :]))
    local_copies, core_copies = [], []
    for i, (w, mine, theirs) in enumerate(places):
        local_copies.append(pltpu.make_async_copy(w.at[0], mine, w_local.at[i]))
        core_copies.append(remote(w.at[0], theirs, w_send.at[i], w_recv.at[i], other_core))
        local_copies[i].start()
        core_copies[i].start()

    row = lax.broadcasted_iota(jnp.int32, (tokens, tokens), 0)
    col = lax.broadcasted_iota(jnp.int32, (tokens, tokens), 1)
    earlier = jnp.where(row < col, 1.0, 0.0).astype(BF16)
    turn = loc + lax.broadcasted_iota(jnp.int32, (8, tokens), 0)
    expert = (half * nh + jnp.where(turn >= nh, turn - nh, turn)).astype(F32)
    slot_id = lax.broadcasted_iota(jnp.int32, (slots, tokens), 0).astype(F32)

    def tables(meta, p):
        for st in range(2):
            i0, i1 = meta[2 * st:2 * st + 1, :], meta[2 * st + 1:2 * st + 2, :]
            p0, p1 = meta[4 + 2 * st:5 + 2 * st, :], meta[5 + 2 * st:6 + 2 * st, :]
            total = p0 + p1
            first, second = i0 == expert, i1 == expert
            named = jnp.where(first, 1.0, jnp.where(second, 1.0, 0.0))
            gate = jnp.where(first, p0 / total, jnp.where(second, p1 / total, 0.0))
            rank = jnp.dot(named.astype(BF16), earlier, preferred_element_type=F32)
            slot = jnp.where(named > 0.5, rank, -1.0)
            weighted = []
            for k in range(nh):
                chosen = jnp.where(slot_id == slot[k:k + 1, :], 1.0, 0.0)
                pick[st, p, pl.ds(k * slots, slots), :] = chosen.astype(BF16)
                weighted.append(chosen * gate[k:k + 1, :])
            flat = jnp.concatenate(weighted, axis=0).T
            top = flat.astype(BF16)
            comb[st, p, 0] = top
            comb[st, p, 1] = (flat - top.astype(F32)).astype(BF16)

    def send_rows(st, p, c, tokens_ref):
        rows = jnp.dot(pick[st, p], tokens_ref[st, c], preferred_element_type=F32).astype(BF16)
        received[st, c, 0, pl.ds(p * slots, slots), :] = rows[:slots]
        for k in range(1, nh):
            outgoing[st, p, c, k] = rows[k * slots:(k + 1) * slots]
            dispatch(st, p, c, k).start()

    def own(st, c):
        relay(st, c).wait_recv()
        to_proxy(st, c).start()
        send_rows(st, 0, c, arrived)

    def proxied(st, c):
        to_proxy(st, c).wait_recv()
        send_rows(st, 1, c, raw)

    def experts(st, k):
        acc_g[...] = jnp.zeros_like(acc_g)
        acc_u[...] = jnp.zeros_like(acc_u)

        @pl.loop(0, nh)
        def _(c):
            @pl.when(k > 0)
            def _():
                dispatch(st, 0, c, k).wait_recv()
                dispatch(st, 1, c, k).wait_recv()

            x = received[st, c, k]
            acc_g[...] += jnp.dot(x, wg[columns(c), :], preferred_element_type=F32)
            acc_u[...] += jnp.dot(x, wu[columns(c), :], preferred_element_type=F32)

        g = acc_g[...]
        hidden[...] = (g / (1.0 + jnp.exp(-g)) * acc_u[...]).astype(BF16)

        @pl.loop(0, nh)
        def _(c):
            y = jnp.dot(hidden[...], wd[:, columns(c)], preferred_element_type=F32).astype(BF16)

            @pl.when(k == 0)
            def _():
                returned[st, 0, c, 0] = y[:slots]
                returned[st, 1, c, 0] = y[slots:]

            @pl.when(k > 0)
            def _():
                received[st, c, k] = y
                give_back(st, 1, c, k).start()
                give_back(st, 0, c, k).start()

    def weighted_sum(st, p, c):
        @pl.loop(1, nh)
        def _(k):
            give_back(st, p, c, k).wait_recv()

        rows = returned[st, p, c].reshape(nh * slots, width)
        return (jnp.dot(comb[st, p, 0], rows, preferred_element_type=F32)
                + jnp.dot(comb[st, p, 1], rows, preferred_element_type=F32))

    def proxy_sum(st, c):
        raw[st, c] = weighted_sum(st, 1, c).astype(BF16)
        from_proxy(st, c).start()

    def finish(st, c):
        total = arrived[st, c].astype(F32) + weighted_sum(st, 0, c)
        from_proxy(st, c).wait_recv()
        outs[st][0, :, columns(c)] = (total + part[st, c].astype(F32)).astype(BF16)

    tables(meta_here[...], 0)
    meta_copy.wait_recv()
    tables(meta_there[...], 1)

    @pl.loop(0, nh)
    def _(c):
        own(0, c)
        relay(1, c).start()

    @pl.loop(0, nh)
    def _(c):
        own(1, c)
        proxied(0, c)

    for i in range(3):
        local_copies[i].wait()
        core_copies[i].wait_recv()

    @pl.loop(0, nh)
    def _(c):
        experts(0, c)
        proxied(1, c)

    @pl.loop(0, nh)
    def _(c):
        experts(1, c)
        proxy_sum(0, c)

    @pl.loop(0, nh)
    def _(c):
        proxy_sum(1, c)
        finish(0, c)

    @pl.loop(0, nh)
    def _(c):
        finish(1, c)

    meta_copy.wait_send()
    for i in range(3):
        core_copies[i].wait_send()

    @pl.loop(0, nh)
    def _(c):
        for st in range(2):
            relay(st, c).wait_send()
            to_proxy(st, c).wait_send()
            from_proxy(st, c).wait_send()
            for p in range(2):
                for k in range(1, nh):
                    dispatch(st, p, c, k).wait_send()
                    give_back(st, p, c, k).wait_send()


def body(act_fwd, act_rev, ids_fwd, ids_rev, probs_fwd, probs_rev, w_gate, w_up, w_down):
    tokens, top = ids_fwd.shape[1:]
    model = act_fwd.shape[2]
    units = w_gate.shape[2]
    experts = lax.axis_size("expert") // 2
    nh = experts // 2
    width = model // nh
    cap = 2 * (3 * tokens * top // (4 * experts))
    slots = -(-cap // 16) * 16
    meta = jnp.concatenate(
        [ids_fwd[0].astype(F32), ids_rev[0].astype(F32), probs_fwd[0], probs_rev[0]], axis=1
    ).T
    anywhere = pl.BlockSpec(memory_space=pl.ANY)
    vmem = pl.BlockSpec(memory_space=pltpu.VMEM)
    dma = pltpu.SemaphoreType.DMA
    out = jax.ShapeDtypeStruct((1, tokens, model), BF16)
    return pl.pallas_call(
        functools.partial(kernel, lax.axis_size("section"), nh, slots, width),
        out_shape=(out, out),
        in_specs=[anywhere, anywhere, vmem, anywhere, anywhere, anywhere],
        out_specs=(vmem, vmem),
        scratch_shapes=[
            pltpu.VMEM((model, 2 * units), BF16),
            pltpu.VMEM((model, 2 * units), BF16),
            pltpu.VMEM((2 * units, model), BF16),
            pltpu.VMEM((8, tokens), F32),
            pltpu.VMEM((2, nh, tokens, width), BF16),
            pltpu.VMEM((2, nh, tokens, width), BF16),
            pltpu.VMEM((2, 2, nh, nh, slots, width), BF16),
            pltpu.VMEM((2, nh, nh, 2 * slots, width), BF16),
            pltpu.VMEM((2, 2, nh, nh, slots, width), BF16),
            pltpu.VMEM((2, nh, tokens, width), BF16),
            pltpu.VMEM((2, 2, nh * slots, tokens), BF16),
            pltpu.VMEM((2, 2, 2, tokens, nh * slots), BF16),
            pltpu.VMEM((2 * slots, 2 * units), F32),
            pltpu.VMEM((2 * slots, 2 * units), F32),
            pltpu.VMEM((2 * slots, 2 * units), BF16),
            dma((3,)), dma((3,)), dma((3,)), dma, dma,
            dma((2, nh)), dma((2, nh)), dma((2, nh)), dma((2, nh)),
            dma((2, 2, nh, nh)), dma((2, 2, nh, nh)), dma((2, 2, nh, nh)), dma((2, 2, nh, nh)),
            dma((2, nh)), dma((2, nh)),
        ],
        compiler_params=pltpu.CompilerParams(
            collective_id=0, has_side_effects=True, vmem_limit_bytes=63 * 1024 * 1024
        ),
        cost_estimate=pl.CostEstimate(
            flops=12 * experts * cap * model * 2 * units,
            bytes_accessed=12 * model * units + 8 * tokens * model,
            transcendentals=0,
        ),
    )(act_fwd, act_rev, meta, w_gate, w_up, w_down)


def solution(mesh):
    return jax.shard_map(
        body,
        mesh=mesh,
        in_specs=(
            P("section", "expert", None),
            P("section", "expert", None),
            P("section", "expert", None),
            P("section", "expert", None),
            P("section", "expert", None),
            P("section", "expert", None),
            P("section", None, "expert"),
            P("section", None, "expert"),
            P("section", "expert", None),
        ),
        out_specs=(P("section", "expert", None), P("section", "expert", None)),
        check_vma=False,
    )
```

time: 337 us -> 267 us (0.79)
  Pallas kernels: 0 us -> 260 us
  waiting for transfers between devices: 234 us -> 0 us
  matrix products: 68.1 us -> 0 us
  starting transfers between devices: 25.1 us -> 0 us
    pallas_call x0 -> x1, Pallas kernels: none -> 260 us  [body(): pl.pallas_call(functools.partial(kernel, lax.axis_size('section'), nh, sl...]
    all_to_all x4 -> x0, waiting for transfers between devices: 188 us -> none  [the longest x2 108 us: moe_layer(): lax.all_to_all(expert_sum.reshape(expert_count, slot_count, model_width),...]
    dot_general x12 -> x0, matrix products: 68.1 us -> none  [the longest x4 37.6 us: half_expert(): jnp.dot(hidden, w_down, preferred_element_type=jnp.float32)]
    ppermute x5 -> x0, waiting for transfers between devices: 46 us -> none  [the longest x2 41.6 us: from_behind(): return lax.ppermute(block, axis, route)]
    all_to_all x4 -> x0, starting transfers between devices: 19.8 us -> none  [the longest x2 10.6 us: moe_layer(): lax.all_to_all(outgoing.reshape(expert_count, slot_count, model_width), '...]
    ppermute x5 -> x0, starting transfers between devices: 5.27 us -> none  [the longest x2 4.62 us: from_behind(): return lax.ppermute(block, axis, route)]
  transfers between devices with their start and end apart: 9 -> 0, of which waited for: 7 -> 0; matrix products, arithmetic and copies ran while one was open for 20% -> 0% of each run, Pallas kernels for 0% -> 0%
where the time goes in v2:
time: 267 us
  Pallas kernels  260 us (97%)
  local copies, waits for them, and re-layouts  4.57 us (2%)
    pallas_call x1, Pallas kernels, body(): pl.pallas_call(functools.partial(kernel, lax.axis_size('section'), nh, sl...  260 us

profile of v2, /device:TPU:0, one launch (start us, length us, event | category | flops | bytes accessed | tf_op | source)
XLA Modules:
  0.0 266.9 jit_solution(13625632675474638447)
XLA Ops:
  0.6 0.7 convert_bitcast_fusion
  1.3 1.3 maximum_bitcast_fusion.meta_here
  2.6 259.7 %shard_map.104 = (bf16[1,128,4096]{2,1,0:T(8,128)(2,1)}, bf16[1,128,4096]{2,1,0:T(8,128)(2,1)}) custom-call(bf16[1,128,4096]{2,1,0:T(8,128)(2,1)} %act_f.1, bf16[1,128,4096]{2,1,0:T(8,128)(2,1)} %act_r.1, f32[8,128]{1,0:T(8,128)} %maximum_bitcast_fusion.meta_here, bf16[1,4096,384]{2,1,0:T(8,128)(2,1)} %w_gate.1, bf16[1,4096,384]{2,1,0:T(8,128)(2,1)} %w_up.1, ...), custom_call_target="tpu_custom_call" | custom-call | flops 14495514624 | bytes 23068672 | tf_op jit(solution)/shard_map/pallas_call | solution.py:258
  262.3 2.3 copy.13
  264.6 2.3 copy.14

commit v3 on v2

v3 whole, which is shorter than its diff:
```python
import functools

import jax
import jax.numpy as jnp
from jax import lax
from jax.experimental import pallas as pl
from jax.experimental.pallas import tpu as pltpu
from jax.sharding import PartitionSpec as P

MESH = pl.DeviceIdType.MESH
F32 = jnp.float32
BF16 = jnp.bfloat16


def kernel(
    sections, nh, slots, width,
    act_f, act_r, meta_here, w_gate, w_up, w_down,
    out_f, out_r,
    wg, wu, wd, meta_there, arrived, raw, out_own, out_proxy, received, returned, part, pick, comb,
    acc_g, acc_u, hidden,
    w_local, w_send, w_recv, meta_send, meta_recv, relay_send, relay_recv, raw_send, raw_recv,
    disp_send, disp_recv, ret_send, ret_recv, part_send, part_recv,
):
    half_units = w_gate.shape[-1]
    tokens = arrived.shape[2]
    nq = nh // 2
    section = lax.axis_index("section")
    me = lax.axis_index("expert")
    core = lax.rem(me, 2)
    chip = me // 2
    half = chip // nh
    loc = lax.rem(chip, nh)
    pos = lax.rem(loc, nq)
    mid = (loc // nq) == (1 - half)
    my_q = jnp.where(mid, 0, 1)
    first_mid = nq * (1 - half)

    def at_chip(c):
        return (section, c * 2 + core)

    def in_half(offset):
        return at_chip(half * nh + lax.rem(loc + offset + nh, nh))

    def mid_peer(j):
        return at_chip(half * nh + first_mid + j)

    proxy = at_chip((1 - half) * nh + nq * half + pos)
    sources = (proxy, at_chip((1 - half) * nh + nq * (1 - half) + pos))
    other_core = (section, chip * 2 + 1 - core)
    after = (lax.rem(section + 1, sections), me)
    before = (lax.rem(section + sections - 1, sections), me)
    acts, outs, ways = (act_f, act_r), (out_f, out_r), (after, before)

    def columns(c):
        return pl.ds(pl.multiple_of(c * width, width), width)

    def remote(src, dst, send, recv, device):
        return pltpu.make_async_remote_copy(
            src_ref=src, dst_ref=dst, send_sem=send, recv_sem=recv,
            device_id=device, device_id_type=MESH,
        )

    def relay(st, c):
        return remote(acts[st].at[0, :, columns(c)], arrived.at[st, c],
                      relay_send.at[st, c], relay_recv.at[st, c], ways[st])

    def to_proxy(st, c, q):
        return remote(arrived.at[st, c], raw.at[st, q, c],
                      raw_send.at[st, c], raw_recv.at[st, q, c], proxy)

    def send_own(st, c, k):
        return remote(out_own.at[st, c, k], received.at[st, 0, c, k],
                      disp_send.at[st, 0, c, k], disp_recv.at[st, 0, c, k], in_half(k))

    def send_proxied(st, q, c, k, block):
        return remote(out_proxy.at[q, c, k], received.at[st, 1, c, block],
                      disp_send.at[st, 1 + q, c, k], disp_recv.at[st, 1, c, block], in_half(k))

    def return_own(st, c, k):
        return remote(received.at[st, 0, c, k], returned.at[st, 0, c, k],
                      ret_send.at[st, 0, c, k], ret_recv.at[st, 0, c, k], in_half(-k))

    def return_proxied(st, q, c, j, k):
        block = 2 * j + q
        return remote(received.at[st, 1, c, block], returned.at[st, 1 + q, c, k],
                      ret_send.at[st, 1, c, block], ret_recv.at[st, 1 + q, c, k], mid_peer(j))

    def from_proxy(st, q, c):
        return remote(raw.at[st, q, c], part.at[st, c],
                      part_send.at[st, q, c], part_recv.at[st, c], sources[q])

    def meta_copy(q):
        return remote(meta_here, meta_there.at[q], meta_send, meta_recv.at[q], proxy)

    barrier = pltpu.get_barrier_semaphore()
    greeted = [after, before, proxy, other_core] + [in_half(k) for k in range(1, nh)]
    for device in greeted:
        pl.semaphore_signal(barrier, inc=1, device_id=device, device_id_type=MESH)

    @pl.when(mid)
    def _():
        for device in sources:
            pl.semaphore_signal(barrier, inc=1, device_id=device, device_id_type=MESH)

    pl.semaphore_wait(barrier, len(greeted) + jnp.where(mid, 2, 0))

    @pl.loop(0, nh)
    def _(c):
        relay(0, c).start()

    meta_copy(my_q).start()

    here, there = pl.ds(0, half_units), pl.ds(half_units, half_units)
    places = ((w_gate, wg.at[:, here], wg.at[:, there]), (w_up, wu.at[:, here], wu.at[:, there]),
              (w_down, wd.at[here, :], wd.at[there, :]))
    local_copies, core_copies = [], []
    for i, (w, mine, theirs) in enumerate(places):
        local_copies.append(pltpu.make_async_copy(w.at[0], mine, w_local.at[i]))
        core_copies.append(remote(w.at[0], theirs, w_send.at[i], w_recv.at[i], other_core))
        local_copies[i].start()
        core_copies[i].start()

    row = lax.broadcasted_iota(jnp.int32, (tokens, tokens), 0)
    col = lax.broadcasted_iota(jnp.int32, (tokens, tokens), 1)
    earlier = jnp.where(row < col, 1.0, 0.0).astype(BF16)
    turn = loc + lax.broadcasted_iota(jnp.int32, (8, tokens), 0)
    expert = (half * nh + jnp.where(turn >= nh, turn - nh, turn)).astype(F32)
    slot_id = lax.broadcasted_iota(jnp.int32, (slots, tokens), 0).astype(F32)

    def tables(meta, p):
        for st in range(2):
            i0, i1 = meta[2 * st:2 * st + 1, :], meta[2 * st + 1:2 * st + 2, :]
            p0, p1 = meta[4 + 2 * st:5 + 2 * st, :], meta[5 + 2 * st:6 + 2 * st, :]
            total = p0 + p1
            first, second = i0 == expert, i1 == expert
            named = jnp.where(first, 1.0, jnp.where(second, 1.0, 0.0))
            gate = jnp.where(first, p0 / total, jnp.where(second, p1 / total, 0.0))
            rank = jnp.dot(named.astype(BF16), earlier, preferred_element_type=F32)
            slot = jnp.where(named > 0.5, rank, -1.0)
            weighted = []
            for k in range(nh):
                chosen = jnp.where(slot_id == slot[k:k + 1, :], 1.0, 0.0)
                pick[st, p, pl.ds(k * slots, slots), :] = chosen.astype(BF16)
                weighted.append(chosen * gate[k:k + 1, :])
            flat = jnp.concatenate(weighted, axis=0).T
            top = flat.astype(BF16)
            comb[st, p, 0] = top
            comb[st, p, 1] = (flat - top.astype(F32)).astype(BF16)

    def own(st, c):
        relay(st, c).wait_recv()
        to_proxy(st, c, my_q).start()
        rows = jnp.dot(pick[st, 0], arrived[st, c], preferred_element_type=F32).astype(BF16)
        received[st, 0, c, 0] = rows[:slots]
        for k in range(1, nh):
            out_own[st, c, k] = rows[k * slots:(k + 1) * slots]
            send_own(st, c, k).start()

    def proxied(st, c):
        for q in range(2):
            to_proxy(st, c, q).wait_recv()
            rows = jnp.dot(pick[st, 1 + q], raw[st, q, c], preferred_element_type=F32).astype(BF16)
            received[st, 1, c, 2 * pos + q] = rows[:slots]
            for k in range(1, nh):
                if st == 1:
                    send_proxied(0, q, c, k, 2 * pos + q).wait_send()
                out_proxy[q, c, k] = rows[k * slots:(k + 1) * slots]
                send_proxied(st, q, c, k, 2 * pos + q).start()

    def experts(st, g):
        acc_g[...] = jnp.zeros_like(acc_g)
        acc_u[...] = jnp.zeros_like(acc_u)

        @pl.loop(0, nh)
        def _(c):
            if g == 0:
                for k in range(1, nh):
                    send_own(st, c, k).wait_recv()
            else:
                for j in range(nq):
                    @pl.when(jnp.logical_not(mid & (pos == j)))
                    def _():
                        for q in range(2):
                            send_proxied(st, q, c, 1, 2 * j + q).wait_recv()

            x = received[st, g, c].reshape(nh * slots, width)
            acc_g[...] += jnp.dot(x, wg[columns(c), :], preferred_element_type=F32)
            acc_u[...] += jnp.dot(x, wu[columns(c), :], preferred_element_type=F32)

        gate = acc_g[...]
        hidden[...] = (gate / (1.0 + jnp.exp(-gate)) * acc_u[...]).astype(BF16)

        @pl.loop(0, nh)
        def _(c):
            y = jnp.dot(hidden[...], wd[:, columns(c)], preferred_element_type=F32).astype(BF16)
            if g == 0:
                returned[st, 0, c, 0] = y[:slots]
                for k in range(1, nh):
                    received[st, 0, c, k] = y[k * slots:(k + 1) * slots]
                    return_own(st, c, k).start()
            else:
                for j in range(nq):
                    blocks = [y[(2 * j + q) * slots:(2 * j + q + 1) * slots] for q in range(2)]
                    myself = mid & (pos == j)

                    @pl.when(myself)
                    def _():
                        for q in range(2):
                            returned[st, 1 + q, c, 0] = blocks[q]

                    @pl.when(jnp.logical_not(myself))
                    def _():
                        offset = lax.rem(loc - first_mid - j + nh, nh)
                        for q in range(2):
                            received[st, 1, c, 2 * j + q] = blocks[q]
                            return_proxied(st, q, c, j, offset).start()

    def weighted_sum(st, p, c):
        rows = returned[st, p, c].reshape(nh * slots, width)
        return (jnp.dot(comb[st, p, 0], rows, preferred_element_type=F32)
                + jnp.dot(comb[st, p, 1], rows, preferred_element_type=F32))

    def proxy_sum(st, c):
        for q in range(2):
            for k in range(1, nh):
                return_proxied(st, q, c, 0, k).wait_recv()
            raw[st, q, c] = weighted_sum(st, 1 + q, c).astype(BF16)
            from_proxy(st, q, c).start()

    def finish(st, c):
        for k in range(1, nh):
            return_own(st, c, k).wait_recv()
        total = arrived[st, c].astype(F32) + weighted_sum(st, 0, c)
        from_proxy(st, 0, c).wait_recv()
        outs[st][0, :, columns(c)] = (total + part[st, c].astype(F32)).astype(BF16)

    tables(meta_here[...], 0)

    @pl.loop(0, nh)
    def _(c):
        own(0, c)
        relay(1, c).start()

    @pl.when(mid)
    def _():
        for q in range(2):
            meta_copy(q).wait_recv()
            tables(meta_there[q], 1 + q)

        @pl.loop(0, nh)
        def _(c):
            proxied(0, c)
            own(1, c)

    @pl.when(jnp.logical_not(mid))
    def _():
        @pl.loop(0, nh)
        def _(c):
            own(1, c)

    for i in range(3):
        local_copies[i].wait()
        core_copies[i].wait_recv()

    experts(0, 0)
    experts(0, 1)

    @pl.when(mid)
    def _():
        @pl.loop(0, nh)
        def _(c):
            proxied(1, c)

    experts(1, 0)

    @pl.when(mid)
    def _():
        @pl.loop(0, nh)
        def _(c):
            proxy_sum(0, c)

    experts(1, 1)

    @pl.when(mid)
    def _():
        @pl.loop(0, nh)
        def _(c):
            proxy_sum(1, c)

    @pl.loop(0, nh)
    def _(c):
        finish(0, c)

    @pl.loop(0, nh)
    def _(c):
        finish(1, c)

    meta_copy(my_q).wait_send()
    for i in range(3):
        core_copies[i].wait_send()

    @pl.loop(0, nh)
    def _(c):
        for st in range(2):
            relay(st, c).wait_send()
            to_proxy(st, c, my_q).wait_send()
            for k in range(1, nh):
                send_own(st, c, k).wait_send()
                return_own(st, c, k).wait_send()
            for j in range(nq):
                @pl.when(jnp.logical_not(mid & (pos == j)))
                def _():
                    for q in range(2):
                        return_proxied(st, q, c, j, 1).wait_send()

    @pl.when(mid)
    def _():
        @pl.loop(0, nh)
        def _(c):
            for q in range(2):
                for st in range(2):
                    from_proxy(st, q, c).wait_send()
                for k in range(1, nh):
                    send_proxied(1, q, c, k, 2 * pos + q).wait_send()


def body(act_fwd, act_rev, ids_fwd, ids_rev, probs_fwd, probs_rev, w_gate, w_up, w_down):
    tokens, top = ids_fwd.shape[1:]
    model = act_fwd.shape[2]
    units = w_gate.shape[2]
    experts = lax.axis_size("expert") // 2
    nh = experts // 2
    width = model // nh
    cap = 2 * (3 * tokens * top // (4 * experts))
    slots = -(-cap // 16) * 16
    meta = jnp.concatenate(
        [ids_fwd[0].astype(F32), ids_rev[0].astype(F32), probs_fwd[0], probs_rev[0]], axis=1
    ).T
    anywhere = pl.BlockSpec(memory_space=pl.ANY)
    vmem = pl.BlockSpec(memory_space=pltpu.VMEM)
    dma = pltpu.SemaphoreType.DMA
    out = jax.ShapeDtypeStruct((1, tokens, model), BF16)
    return pl.pallas_call(
        functools.partial(kernel, lax.axis_size("section"), nh, slots, width),
        out_shape=(out, out),
        in_specs=[anywhere, anywhere, vmem, anywhere, anywhere, anywhere],
        out_specs=(vmem, vmem),
        scratch_shapes=[
            pltpu.VMEM((model, 2 * units), BF16),
            pltpu.VMEM((model, 2 * units), BF16),
            pltpu.VMEM((2 * units, model), BF16),
            pltpu.VMEM((2, 8, tokens), F32),
            pltpu.VMEM((2, nh, tokens, width), BF16),
            pltpu.VMEM((2, 2, nh, tokens, width), BF16),
            pltpu.VMEM((2, nh, nh, slots, width), BF16),
            pltpu.VMEM((2, nh, nh, slots, width), BF16),
            pltpu.VMEM((2, 2, nh, nh, slots, width), BF16),
            pltpu.VMEM((2, 3, nh, nh, slots, width), BF16),
            pltpu.VMEM((2, nh, tokens, width), BF16),
            pltpu.VMEM((2, 3, nh * slots, tokens), BF16),
            pltpu.VMEM((2, 3, 2, tokens, nh * slots), BF16),
            pltpu.VMEM((nh * slots, 2 * units), F32),
            pltpu.VMEM((nh * slots, 2 * units), F32),
            pltpu.VMEM((nh * slots, 2 * units), BF16),
            dma((3,)), dma((3,)), dma((3,)), dma, dma((2,)),
            dma((2, nh)), dma((2, nh)), dma((2, nh)), dma((2, 2, nh)),
            dma((2, 3, nh, nh)), dma((2, 2, nh, nh)), dma((2, 2, nh, nh)), dma((2, 3, nh, nh)),
            dma((2, 2, nh)), dma((2, nh)),
        ],
        compiler_params=pltpu.CompilerParams(
            collective_id=0, has_side_effects=True, vmem_limit_bytes=63 * 1024 * 1024
        ),
        cost_estimate=pl.CostEstimate(
            flops=12 * experts * cap * model * 2 * units,
            bytes_accessed=12 * model * units + 8 * tokens * model,
            transcendentals=0,
        ),
    )(act_fwd, act_rev, meta, w_gate, w_up, w_down)


def solution(mesh):
    return jax.shard_map(
        body,
        mesh=mesh,
        in_specs=(
            P("section", "expert", None),
            P("section", "expert", None),
            P("section", "expert", None),
            P("section", "expert", None),
            P("section", "expert", None),
            P("section", "expert", None),
            P("section", None, "expert"),
            P("section", None, "expert"),
            P("section", "expert", None),
        ),
        out_specs=(P("section", "expert", None), P("section", "expert", None)),
        check_vma=False,
    )
```

time: 267 us -> 238 us (0.89)
  Pallas kernels: 260 us -> 230 us
    pallas_call x1, Pallas kernels: 260 us -> 230 us  [body(): pl.pallas_call(functools.partial(kernel, lax.axis_size('section'), nh, sl...]
where the time goes in v3:
time: 238 us
  Pallas kernels  230 us (97%)
  local copies, waits for them, and re-layouts  4.57 us (2%)
    pallas_call x1, Pallas kernels, body(): pl.pallas_call(functools.partial(kernel, lax.axis_size('section'), nh, sl...  230 us

profile of v3, /device:TPU:0, one launch (start us, length us, event | category | flops | bytes accessed | tf_op | source)
XLA Modules:
  0.0 237.6 jit_solution(15297277361410943261)
XLA Ops:
  0.6 0.7 convert_bitcast_fusion
  1.3 1.3 maximum_bitcast_fusion.meta_here
  2.6 230.4 %shard_map.104 = (bf16[1,128,4096]{2,1,0:T(8,128)(2,1)}, bf16[1,128,4096]{2,1,0:T(8,128)(2,1)}) custom-call(bf16[1,128,4096]{2,1,0:T(8,128)(2,1)} %act_f.1, bf16[1,128,4096]{2,1,0:T(8,128)(2,1)} %act_r.1, f32[8,128]{1,0:T(8,128)} %maximum_bitcast_fusion.meta_here, bf16[1,4096,384]{2,1,0:T(8,128)(2,1)} %w_gate.1, bf16[1,4096,384]{2,1,0:T(8,128)(2,1)} %w_up.1, ...), custom_call_target="tpu_custom_call" | custom-call | flops 14495514624 | bytes 23068672 | tf_op jit(solution)/shard_map/pallas_call | solution.py:343
  233.0 2.3 copy.13
  235.3 2.3 copy.14

commit v4 on v3

--- a/solution.py
+++ b/solution.py
@@ -263,23 +263,31 @@
         core_copies[i].wait_recv()
 
     experts(0, 0)
+    experts(1, 0)
+
+    @pl.when(mid)
+    def _():
+        proxied(1, 0)
+
     experts(0, 1)
 
     @pl.when(mid)
     def _():
-        @pl.loop(0, nh)
+        @pl.loop(1, nh)
         def _(c):
             proxied(1, c)
 
-    experts(1, 0)
-
-    @pl.when(mid)
-    def _():
-        @pl.loop(0, nh)
+        @pl.loop(0, nq)
         def _(c):
             proxy_sum(0, c)
 
     experts(1, 1)
+
+    @pl.when(mid)
+    def _():
+        @pl.loop(nq, nh)
+        def _(c):
+            proxy_sum(0, c)
 
     @pl.when(mid)
     def _():

time: 238 us -> 255 us (1.071)
  Pallas kernels: 230 us -> 247 us
    pallas_call x1, Pallas kernels: 230 us -> 247 us  [body(): pl.pallas_call(functools.partial(kernel, lax.axis_size('section'), nh, sl...]
where the time goes in v4:
time: 255 us
  Pallas kernels  247 us (97%)
  local copies, waits for them, and re-layouts  4.57 us (2%)
    pallas_call x1, Pallas kernels, body(): pl.pallas_call(functools.partial(kernel, lax.axis_size('section'), nh, sl...  247 us

profile of v4, /device:TPU:0, one launch (start us, length us, event | category | flops | bytes accessed | tf_op | source)
XLA Modules:
  0.0 254.7 jit_solution(1393061050996796100)
XLA Ops:
  0.6 0.7 convert_bitcast_fusion
  1.3 1.3 maximum_bitcast_fusion.meta_here
  2.6 247.5 %shard_map.104 = (bf16[1,128,4096]{2,1,0:T(8,128)(2,1)}, bf16[1,128,4096]{2,1,0:T(8,128)(2,1)}) custom-call(bf16[1,128,4096]{2,1,0:T(8,128)(2,1)} %act_f.1, bf16[1,128,4096]{2,1,0:T(8,128)(2,1)} %act_r.1, f32[8,128]{1,0:T(8,128)} %maximum_bitcast_fusion.meta_here, bf16[1,4096,384]{2,1,0:T(8,128)(2,1)} %w_gate.1, bf16[1,4096,384]{2,1,0:T(8,128)(2,1)} %w_up.1, ...), custom_call_target="tpu_custom_call" | custom-call | flops 14495514624 | bytes 23068672 | tf_op jit(solution)/shard_map/pallas_call | solution.py:351
  250.1 2.3 copy.13
  252.4 2.3 copy.14

commit v5 on v3

--- a/solution.py
+++ b/solution.py
@@ -250,10 +250,7 @@
         @pl.loop(0, nh)
         def _(c):
             proxied(0, c)
-            own(1, c)
-
-    @pl.when(jnp.logical_not(mid))
-    def _():
+
         @pl.loop(0, nh)
         def _(c):
             own(1, c)
@@ -263,6 +260,13 @@
         core_copies[i].wait_recv()
 
     experts(0, 0)
+
+    @pl.when(jnp.logical_not(mid))
+    def _():
+        @pl.loop(0, nh)
+        def _(c):
+            own(1, c)
+
     experts(0, 1)
 
     @pl.when(mid)

time: 238 us -> 229 us (0.962)
  Pallas kernels: 230 us -> 222 us
    pallas_call x1, Pallas kernels: 230 us -> 222 us  [body(): pl.pallas_call(functools.partial(kernel, lax.axis_size('section'), nh, sl...]
where the time goes in v5:
time: 229 us
  Pallas kernels  222 us (97%)
  local copies, waits for them, and re-layouts  4.57 us (2%)
    pallas_call x1, Pallas kernels, body(): pl.pallas_call(functools.partial(kernel, lax.axis_size('section'), nh, sl...  222 us

profile of v5, /device:TPU:0, one launch (start us, length us, event | category | flops | bytes accessed | tf_op | source)
XLA Modules:
  0.0 228.8 jit_solution(12707188319701949270)
XLA Ops:
  0.6 0.7 convert_bitcast_fusion
  1.3 1.3 maximum_bitcast_fusion.meta_here
  2.6 221.6 %shard_map.104 = (bf16[1,128,4096]{2,1,0:T(8,128)(2,1)}, bf16[1,128,4096]{2,1,0:T(8,128)(2,1)}) custom-call(bf16[1,128,4096]{2,1,0:T(8,128)(2,1)} %act_f.1, bf16[1,128,4096]{2,1,0:T(8,128)(2,1)} %act_r.1, f32[8,128]{1,0:T(8,128)} %maximum_bitcast_fusion.meta_here, bf16[1,4096,384]{2,1,0:T(8,128)(2,1)} %w_gate.1, bf16[1,4096,384]{2,1,0:T(8,128)(2,1)} %w_up.1, ...), custom_call_target="tpu_custom_call" | custom-call | flops 14495514624 | bytes 23068672 | tf_op jit(solution)/shard_map/pallas_call | solution.py:347
  224.2 2.3 %copy.13 = bf16[1,128,4096]{2,1,0:T(8,128)(2,1)} copy(bf16[1,128,4096]{2,1,0:T(8,128)(2,1)} %get-tuple-element.6) | data formatting | bytes 2097152
  226.5 2.3 copy.14

commit v6 on v5

--- a/solution.py
+++ b/solution.py
@@ -104,8 +104,7 @@
 
     pl.semaphore_wait(barrier, len(greeted) + jnp.where(mid, 2, 0))
 
-    @pl.loop(0, nh)
-    def _(c):
+    for c in range(2):
         relay(0, c).start()
 
     meta_copy(my_q).start()
@@ -150,6 +149,15 @@
     def own(st, c):
         relay(st, c).wait_recv()
         to_proxy(st, c, my_q).start()
+        if st == 0:
+            @pl.when(c < nh - 2)
+            def _():
+                relay(0, c + 2).start()
+
+            @pl.when(c >= nh - 2)
+            def _():
+                relay(1, c - (nh - 2)).start()
+
         rows = jnp.dot(pick[st, 0], arrived[st, c], preferred_element_type=F32).astype(BF16)
         received[st, 0, c, 0] = rows[:slots]
         for k in range(1, nh):
@@ -239,6 +247,9 @@
     @pl.loop(0, nh)
     def _(c):
         own(0, c)
+
+    @pl.loop(2, nh)
+    def _(c):
         relay(1, c).start()
 
     @pl.when(mid)

time: 229 us -> 229 us (level)
  no operation moved by 1% of the time
where the time goes in v6:
time: 229 us
  Pallas kernels  222 us (97%)
  local copies, waits for them, and re-layouts  4.57 us (2%)
    pallas_call x1, Pallas kernels, body(): pl.pallas_call(functools.partial(kernel, lax.axis_size('section'), nh, sl...  222 us

profile of v6, /device:TPU:0, one launch (start us, length us, event | category | flops | bytes accessed | tf_op | source)
XLA Modules:
  0.0 228.7 jit_solution(451208116572378061)
XLA Ops:
  0.6 0.7 convert_bitcast_fusion
  1.3 1.3 maximum_bitcast_fusion.meta_here
  2.6 221.5 %shard_map.104 = (bf16[1,128,4096]{2,1,0:T(8,128)(2,1)}, bf16[1,128,4096]{2,1,0:T(8,128)(2,1)}) custom-call(bf16[1,128,4096]{2,1,0:T(8,128)(2,1)} %act_f.1, bf16[1,128,4096]{2,1,0:T(8,128)(2,1)} %act_r.1, f32[8,128]{1,0:T(8,128)} %maximum_bitcast_fusion.meta_here, bf16[1,4096,384]{2,1,0:T(8,128)(2,1)} %w_gate.1, bf16[1,4096,384]{2,1,0:T(8,128)(2,1)} %w_up.1, ...), custom_call_target="tpu_custom_call" | custom-call | flops 14495514624 | bytes 23068672 | tf_op jit(solution)/shard_map/pallas_call | solution.py:358
  224.2 2.3 %copy.13 = bf16[1,128,4096]{2,1,0:T(8,128)(2,1)} copy(bf16[1,128,4096]{2,1,0:T(8,128)(2,1)} %get-tuple-element.6) | data formatting | bytes 2097152
  226.5 2.3 copy.14
